TPU v7x, 32 devices: a whole 2x2x4 slice. The times are simulated.
32 devices in a mesh: groups: 1, dom: 8 (over z, y), chan: 2 (over x), sub: 2 (over core).
Axes of the slice: x: 2, y: 2, z: 4, core: 2. Of those that a mesh axis runs over, the one named last changes fastest.
Arguments:
- y_last: bfloat16 [2, 128, 8192], P(None, 'chan', ('groups', 'dom', 'sub')), may hold values from -6 to 6
- dy_last: bfloat16 [2, 128, 8192], P(None, 'chan', ('groups', 'dom', 'sub')), may hold values from -6 to 6
- weights: bfloat16 [2, 2, 128, 128], replicated, may hold values from -0.5 to 0.5
- tile_vals: bfloat16 [64, 8, 128, 128], P(('groups', 'dom', 'sub')), may hold values from -0.1875 to 0.1875
- tile_cols: int32 [64, 8], P(('groups', 'dom', 'sub')), may hold values from 0 to 7, as said below
- tile_mask: int32 [64, 8], P(('groups', 'dom', 'sub')), may hold values from 0 to 1, as said below
- send_rows: int32 [16, 16, 32], P(('groups', 'dom', 'sub')), may hold values from 0 to 511, as said below
- send_count: int32 [16, 16], P(('groups', 'dom', 'sub')), may hold values from 0 to 32, as said below
Outputs:
- input_grads: bfloat16 [2, 128, 8192], P(None, 'chan', ('groups', 'dom', 'sub'))
- weight_grads: float32 [2, 2, 128, 128], P('groups', None, 'chan')
Inputs may be any that keep to these rules, and one draw needn't show every extreme that they name: The 8 entries of one row of tile_cols are distinct; slot 0 of row q * 4 + r names column block r, the block's own rows. `tile_mask`: in each row the live slots come first and slot 0 is live. The first send_count[p, q] entries of send_rows[p, q] are distinct. send_count[p, p] is 0; in every draw some block q receives 32 rows from every other block.
All inputs are finite; a program needn't handle non-finite values.
Results may differ from a plain program's by a relative error of at most 0.0085.
Values may be sent and summed in bfloat16 or wider, within the bound.
A program may use at most 64 MiB of HBM per device.

v0:
```python
import math

import jax
import jax.numpy as jnp
from jax import lax
from jax.sharding import PartitionSpec as P


def silu_slope(value):
    sigmoid = jax.nn.sigmoid(value)
    return sigmoid * (1.0 + value * (1.0 - sigmoid))


def live_slots(send_count, send_rows):
    return jnp.arange(send_rows.shape[2], dtype=jnp.int32)[None, :] < send_count[0][:, None]


def send_halo(feature, send_rows, live_mask):
    channels = feature.shape[0]
    picked = feature[:, send_rows[0]]
    picked = jnp.where(live_mask[None], picked, jnp.zeros_like(picked))
    outgoing = picked.reshape(channels, -1)
    arrived = lax.all_to_all(outgoing, ("dom", "sub"), split_axis=1, concat_axis=1, tiled=True)
    return arrived


def propagate(feature, halo_part, tile_vals, tile_cols, tile_mask):
    channels, own_rows = feature.shape
    tile_size = tile_vals.shape[-1]
    extended = jnp.concatenate([feature, halo_part], axis=1).reshape(channels, -1, tile_size)
    picked = extended[:, tile_cols]
    picked = picked * tile_mask[None, :, :, None].astype(picked.dtype)
    result = jnp.einsum("crkj,rkji->cri", picked, tile_vals, preferred_element_type=jnp.float32)
    return result.reshape(channels, own_rows)


def propagate_back(gradient, tile_vals, tile_cols, tile_mask, send_rows, live_mask):
    channels, own_rows = gradient.shape
    tile_size = tile_vals.shape[-1]
    row_blocks, tile_slots = tile_cols.shape
    halo_width = send_rows.shape[1] * send_rows.shape[2]
    col_blocks = (own_rows + halo_width) // tile_size
    shaped = gradient.reshape(channels, row_blocks, tile_size)
    terms = jnp.einsum("cri,rkji->crkj", shaped, tile_vals, preferred_element_type=jnp.float32)
    terms = terms * tile_mask[None, :, :, None].astype(jnp.float32)
    totals = jnp.zeros((channels, col_blocks, tile_size), jnp.float32)
    totals = totals.at[:, tile_cols.reshape(-1)].add(
        terms.reshape(channels, row_blocks * tile_slots, tile_size)
    )
    totals = totals.reshape(channels, -1)
    local_part = totals[:, :own_rows]
    outgoing = totals[:, own_rows:]
    returned = lax.all_to_all(outgoing, ("dom", "sub"), split_axis=1, concat_axis=1, tiled=True)
    returned = returned.reshape(channels, live_mask.shape[0], live_mask.shape[1])
    returned = jnp.where(live_mask[None], returned, 0.0)
    return local_part.at[:, send_rows[0].reshape(-1)].add(returned.reshape(channels, -1))


def mix_forward(message, weight):
    channels, own_rows = message.shape
    offset_own = lax.axis_index("chan") * channels
    columns = lax.dynamic_slice_in_dim(weight, offset_own, channels, 1)

    def accumulate(running, incoming, offset):
        return jnp.einsum("io,ir->or", columns, incoming, preferred_element_type=jnp.float32)

    initial = jnp.zeros((channels, own_rows), jnp.float32)
    return accumulate(initial, lax.all_gather(message, "chan", axis=0, tiled=True), jnp.int32(0))


def mix_backward(slope, message, weight):
    channels, own_rows = slope.shape
    offset_own = lax.axis_index("chan") * channels
    weight_rows = lax.dynamic_slice_in_dim(weight, offset_own, channels, 0)

    def accumulate(running, incoming, offset):
        moved = jnp.dot(weight_rows, incoming, preferred_element_type=jnp.float32)
        outer = jnp.einsum("ir,or->io", message, incoming, preferred_element_type=jnp.float32)
        return (moved, outer)

    initial = (
        jnp.zeros((channels, own_rows), jnp.float32),
        jnp.zeros((channels, weight.shape[1]), jnp.float32),
    )
    return accumulate(initial, lax.all_gather(slope, "chan", axis=0, tiled=True), jnp.int32(0))


def on_device(y_last, dy_last, weights, tile_vals, tile_cols, tile_mask, send_rows, send_count):
    live_mask = live_slots(send_count, send_rows)
    own_rows = y_last.shape[2]
    total_rows = own_rows * lax.axis_size("dom") * lax.axis_size("sub")
    factor = 1.0 / math.sqrt(total_rows)

    def forward_pass(feature):
        return propagate(
            feature, send_halo(feature, send_rows, live_mask), tile_vals, tile_cols, tile_mask
        )

    def backward_pass(gradient):
        return propagate_back(gradient, tile_vals, tile_cols, tile_mask, send_rows, live_mask)

    state_one = y_last[0]
    state_two = y_last[1]
    grad_one = dy_last[0].astype(jnp.float32)
    grad_two = dy_last[1].astype(jnp.float32)
    collected = []
    for layer_index in reversed(range(weights.shape[0])):
        first = weights[layer_index, 0]
        second = weights[layer_index, 1]
        message_two = forward_pass(state_one).astype(jnp.bfloat16)
        linear_two = mix_forward(message_two, second)
        input_two = (state_two.astype(jnp.float32) - jax.nn.silu(linear_two)).astype(jnp.bfloat16)
        message_one = forward_pass(input_two).astype(jnp.bfloat16)
        linear_one = mix_forward(message_one, first)
        slope_two = (grad_two * silu_slope(linear_two)).astype(jnp.bfloat16)
        back_two, weight_two = mix_backward(slope_two, message_two, second)
        grad_one = grad_one + backward_pass(back_two.astype(jnp.bfloat16))
        slope_one = (grad_one * silu_slope(linear_one)).astype(jnp.bfloat16)
        back_one, weight_one = mix_backward(slope_one, message_one, first)
        grad_two = grad_two + backward_pass(back_one.astype(jnp.bfloat16))
        weight_one, weight_two = lax.psum((weight_one, weight_two), ("dom", "sub"))
        collected.insert(0, jnp.stack([weight_one, weight_two]))
        if layer_index > 0:
            state_one = (state_one.astype(jnp.float32) - jax.nn.silu(linear_one)).astype(
                jnp.bfloat16
            )
            state_two = input_two
    stacked = jnp.stack(collected)
    input_grads = jnp.stack([grad_one, grad_two]).astype(jnp.bfloat16)
    return (input_grads, stacked * factor)


def solution(mesh):
    return jax.shard_map(
        on_device,
        mesh=mesh,
        in_specs=(
            P(None, "chan", ("groups", "dom", "sub")),
            P(None, "chan", ("groups", "dom", "sub")),
            P(),
            P(("groups", "dom", "sub"), None, None, None),
            P(("groups", "dom", "sub"), None),
            P(("groups", "dom", "sub"), None),
            P(("groups", "dom", "sub"), None, None),
            P(("groups", "dom", "sub"), None),
        ),
        out_specs=(P(None, "chan", ("groups", "dom", "sub")), P("groups", None, "chan", None)),
        check_vma=False,
    )
```

profile of v0, /device:TPU:0, one launch (start us, length us, event | category | flops | bytes accessed | tf_op | source)
XLA Modules:
  0.0 254.4 jit_solution(16756262767047960695)
XLA Ops:
  12.0 7.5 %all-to-all-start = ((bf16[16,2,1024]{2,1,0:T(2,128)(2,1)}), bf16[16,2,1024]{2,1,0:T(2,128)(2,1)S(1)}, u32[]{:S(2)}, u32[]{:S(2)}) async-start(bf16[16,2,1024]{2,1,0:T(2,128)(2,1)} %reshape.444), calls=%async_computation | async-start | bytes 131072 | tf_op jit(solution)/shard_map/all_to_all | solution.py:23
  22.5 4.0 %all-to-all-done = bf16[16,2,1024]{2,1,0:T(2,128)(2,1)S(1)} async-done(((bf16[16,2,1024]{2,1,0:T(2,128)(2,1)}), bf16[16,2,1024]{2,1,0:T(2,128)(2,1)S(1)}, u32[]{:S(2)}, u32[]{:S(2)}) %all-to-all-start) | async-done | bytes 65568 | tf_op jit(solution)/shard_map/all_to_all | solution.py:23
  27.8 5.1 %all_gather.24 = bf16[128,512]{1,0:T(8,128)(2,1)S(1)} all-gather(bf16[64,512]{1,0:T(8,128)(2,1)S(1)} %bitcast.310), channel_id=1, replica_groups=mesh['groups'=1,'dom'=8,'chan'=2,'sub'=2] {'chan'}, dimensions={0}, use_global_device_ids=true | all-gather | bytes 196608 | tf_op jit(solution)/shard_map/all_gather | solution.py:68
  33.2 4.9 %all_gather.25 = bf16[128,512]{1,0:T(8,128)(2,1)S(1)} all-gather(bf16[64,512]{1,0:T(8,128)(2,1)S(1)} %get-tuple-element.29), channel_id=1, replica_groups=mesh['groups'=1,'dom'=8,'chan'=2,'sub'=2] {'chan'}, dimensions={0}, use_global_device_ids=true | all-gather | bytes 196608 | tf_op jit(solution)/shard_map/all_gather | solution.py:85
  40.7 3.5 %all-to-all-start.2 = ((bf16[16,2,1024]{2,1,0:T(2,128)(2,1)}), bf16[16,2,1024]{2,1,0:T(2,128)(2,1)S(1)}, u32[]{:S(2)}, u32[]{:S(2)}) async-start(bf16[16,2,1024]{2,1,0:T(2,128)(2,1)} %reshape.448), calls=%async_computation.2 | async-start | bytes 131072 | tf_op jit(solution)/shard_map/all_to_all | solution.py:23
  48.9 2.2 all-to-all-done.2
  51.1 3.7 %all-to-all-start.1 = ((f32[16,1,2048]{2,1,0:T(1,128)}), f32[16,1,2048]{2,1,0:T(1,128)S(1)}, u32[]{:S(2)}, u32[]{:S(2)}) async-start(f32[16,1,2048]{2,1,0:T(1,128)} %reshape.446), calls=%async_computation.1 | async-start | bytes 262144 | tf_op jit(solution)/shard_map/all_to_all | solution.py:53
  56.2 5.1 %all_gather.26 = bf16[128,512]{1,0:T(8,128)(2,1)S(1)} all-gather(bf16[64,512]{1,0:T(8,128)(2,1)S(1)} %bitcast.311), channel_id=1, replica_groups=mesh['groups'=1,'dom'=8,'chan'=2,'sub'=2] {'chan'}, dimensions={0}, use_global_device_ids=true | all-gather | bytes 196608 | tf_op jit(solution)/shard_map/all_gather | solution.py:68
  64.5 3.4 %scatter_custom_fusion.1 = f32[64,512]{0,1:T(8,128)S(1)} fusion(f32[64,512]{0,1:T(8,128)S(1)} %get-tuple-element.34, s32[512]{0:T(512)S(1)} %bitcast.316, f32[64,512]{0,1:T(8,128)S(1)} %get-tuple-element.35), kind=kCustom, calls=%fused_computation.63 | custom fusion | flops 32768 | bytes 393216 | tf_op jit(solution)/shard_map/scatter-add | solution.py:56
  69.2 4.9 %all_gather.27 = bf16[128,512]{1,0:T(8,128)(2,1)S(1)} all-gather(bf16[64,512]{1,0:T(8,128)(2,1)S(1)} %get-tuple-element.27), channel_id=1, replica_groups=mesh['groups'=1,'dom'=8,'chan'=2,'sub'=2] {'chan'}, dimensions={0}, use_global_device_ids=true | all-gather | bytes 196608 | tf_op jit(solution)/shard_map/all_gather | solution.py:85
  76.7 4.3 %all-to-all-start.4 = ((bf16[16,2,1024]{2,1,0:T(2,128)(2,1)}), bf16[16,2,1024]{2,1,0:T(2,128)(2,1)S(1)}, u32[]{:S(2)}, u32[]{:S(2)}) async-start(bf16[16,2,1024]{2,1,0:T(2,128)(2,1)} %reshape.452), calls=%async_computation.4 | async-start | bytes 131072 | tf_op jit(solution)/shard_map/all_to_all | solution.py:23
  88.0 4.4 %all-to-all-start.3 = ((f32[16,1,2048]{2,1,0:T(1,128)}), f32[16,1,2048]{2,1,0:T(1,128)S(1)}, u32[]{:S(2)}, u32[]{:S(2)}) async-start(f32[16,1,2048]{2,1,0:T(1,128)} %reshape.450), calls=%async_computation.3 | async-start | bytes 262144 | tf_op jit(solution)/shard_map/all_to_all | solution.py:53
  94.3 5.1 %all_gather.28 = bf16[128,512]{1,0:T(8,128)(2,1)S(1)} all-gather(bf16[64,512]{1,0:T(8,128)(2,1)S(1)} %bitcast.312), channel_id=1, replica_groups=mesh['groups'=1,'dom'=8,'chan'=2,'sub'=2] {'chan'}, dimensions={0}, use_global_device_ids=true | all-gather | bytes 196608 | tf_op jit(solution)/shard_map/all_gather | solution.py:68
  102.1 3.6 %scatter_custom_fusion.3 = f32[64,512]{0,1:T(8,128)S(1)} fusion(f32[64,512]{0,1:T(8,128)S(1)} %copy.86, s32[512]{0:T(512)} %bitcast.317, f32[64,512]{0,1:T(8,128)S(1)} %bitcast_select_fusion.2), kind=kCustom, calls=%fused_computation.60 | custom fusion | flops 32768 | bytes 393216 | tf_op jit(solution)/shard_map/scatter-add | solution.py:56
  106.7 4.9 %all_gather.29 = bf16[128,512]{1,0:T(8,128)(2,1)S(1)} all-gather(bf16[64,512]{1,0:T(8,128)(2,1)S(1)} %get-tuple-element.25), channel_id=1, replica_groups=mesh['groups'=1,'dom'=8,'chan'=2,'sub'=2] {'chan'}, dimensions={0}, use_global_device_ids=true | all-gather | bytes 196608 | tf_op jit(solution)/shard_map/all_gather | solution.py:85
  114.2 5.0 %all-to-all-start.6 = ((bf16[16,2,1024]{2,1,0:T(2,128)(2,1)}), bf16[16,2,1024]{2,1,0:T(2,128)(2,1)S(1)}, u32[]{:S(2)}, u32[]{:S(2)}) async-start(bf16[16,2,1024]{2,1,0:T(2,128)(2,1)} %reshape.456), calls=%async_computation.6 | async-start | bytes 131072 | tf_op jit(solution)/shard_map/all_to_all | solution.py:23
  126.1 4.3 %all-to-all-start.5 = ((f32[16,1,2048]{2,1,0:T(1,128)}), f32[16,1,2048]{2,1,0:T(1,128)S(1)}, u32[]{:S(2)}, u32[]{:S(2)}) async-start(f32[16,1,2048]{2,1,0:T(1,128)} %reshape.454), calls=%async_computation.5 | async-start | bytes 262144 | tf_op jit(solution)/shard_map/all_to_all | solution.py:53
  131.8 5.1 %all_gather.30 = bf16[128,512]{1,0:T(8,128)(2,1)S(1)} all-gather(bf16[64,512]{1,0:T(8,128)(2,1)S(1)} %bitcast.313), channel_id=1, replica_groups=mesh['groups'=1,'dom'=8,'chan'=2,'sub'=2] {'chan'}, dimensions={0}, use_global_device_ids=true | all-gather | bytes 196608 | tf_op jit(solution)/shard_map/all_gather | solution.py:68
  139.5 3.6 %scatter_custom_fusion.5 = f32[64,512]{0,1:T(8,128)S(1)} fusion(f32[64,512]{0,1:T(8,128)S(1)} %get-tuple-element.15, s32[512]{0:T(512)} %bitcast.318, f32[64,512]{0,1:T(8,128)S(1)} %bitcast_select_fusion.1), kind=kCustom, calls=%fused_computation.57 | custom fusion | flops 32768 | bytes 393216 | tf_op jit(solution)/shard_map/scatter-add | solution.py:56
  144.2 4.9 %all_gather.31 = bf16[128,512]{1,0:T(8,128)(2,1)S(1)} all-gather(bf16[64,512]{1,0:T(8,128)(2,1)S(1)} %multiply_convert_fusion), channel_id=1, replica_groups=mesh['groups'=1,'dom'=8,'chan'=2,'sub'=2] {'chan'}, dimensions={0}, use_global_device_ids=true | all-gather | bytes 196608 | tf_op jit(solution)/shard_map/all_gather | solution.py:85
  150.6 2.1 scatter_fusion.3
  153.9 4.4 %all-to-all-start.7 = ((f32[16,1,2048]{2,1,0:T(1,128)}), f32[16,1,2048]{2,1,0:T(1,128)S(1)}, u32[]{:S(2)}, u32[]{:S(2)}) async-start(f32[16,1,2048]{2,1,0:T(1,128)} %reshape.458), calls=%async_computation.7 | async-start | bytes 262144 | tf_op jit(solution)/shard_map/all_to_all | solution.py:53
  158.3 82.2 %all-reduce.3.cloned.1.call-done = (f32[1,64,128]{2,1,0:T(8,128)}, f32[1,64,128]{2,1,0:T(8,128)}, f32[1,64,128]{2,1,0:T(8,128)}, f32[1,64,128]{2,1,0:T(8,128)}) async-done(((f32[1,64,128]{2,1,0:T(8,128)}, f32[1,64,128]{2,1,0:T(8,128)}, f32[1,64,128]{2,1,0:T(8,128)}, f32[1,64,128]{2,1,0:T(8,128)}), (f32[1,64,128]{2,1,0:T(8,128)}, f32[1,64,128]{2,1,0:T(8,128)}, f32[1,64,128]{2,1,0:T(8,128)}, ...) | async-done | bytes 131088 | tf_op jit(solution)/shard_map/psum | solution.py:121
  243.1 3.6 %scatter_custom_fusion.7 = f32[64,512]{0,1:T(8,128)S(1)} fusion(f32[64,512]{0,1:T(8,128)S(1)} %get-tuple-element.13, s32[512]{0:T(512)} %bitcast.319, f32[64,512]{0,1:T(8,128)S(1)} %bitcast_select_fusion), kind=kCustom, calls=%fused_computation.54 | custom fusion | flops 32768 | bytes 393216 | tf_op jit(solution)/shard_map/scatter-add | solution.py:56
  (185 shorter events, 57.4 us)
Async XLA Ops:
  7.2 20.2 %copy-start = (bf16[4,8,128,128]{3,2,1,0:T(8,128)(2,1)S(1)}, bf16[4,8,128,128]{3,2,1,0:T(8,128)(2,1)}, u32[]{:S(2)}) copy-start(bf16[4,8,128,128]{3,2,1,0:T(8,128)(2,1)} %param.11) | copy-start | bytes 3145732
  11.3 9.2 %copy-start.2 = (bf16[2,2,128,128]{3,2,1,0:T(8,128)(2,1)S(1)}, bf16[2,2,128,128]{3,2,1,0:T(8,128)(2,1)}, u32[]{:S(2)}) copy-start(bf16[2,2,128,128]{3,2,1,0:T(8,128)(2,1)} %param.10) | copy-start | bytes 393220
  12.0 7.5 %copy-start.13 = (s32[4,8]{1,0:T(4,128)S(1)}, s32[4,8]{1,0:T(4,128)}, u32[]{:S(2)}) copy-start(s32[4,8]{1,0:T(4,128)} %param.12) | copy-start | bytes 388
  12.0 7.6 %copy-start.8 = (s32[1,16,32]{2,1,0:T(8,128)S(1)}, s32[1,16,32]{2,1,0:T(8,128)}, u32[]{:S(2)}) copy-start(s32[1,16,32]{2,1,0:T(8,128)} %param.14) | copy-start | bytes 6148
  12.0 14.4 %all-to-all-start = ((bf16[16,2,1024]{2,1,0:T(2,128)(2,1)}), bf16[16,2,1024]{2,1,0:T(2,128)(2,1)S(1)}, u32[]{:S(2)}, u32[]{:S(2)}) async-start(bf16[16,2,1024]{2,1,0:T(2,128)(2,1)} %reshape.444), calls=%async_computation | async-start | bytes 131072 | tf_op jit(solution)/shard_map/all_to_all | solution.py:23
  19.7 25.0 %copy-start.14 = (s32[32]{0:T(128)}, s32[32]{0:T(128)S(1)}, u32[]{:S(2)}) copy-start(s32[32]{0:T(128)S(1)} %fusion.64) | copy-start | bytes 388
  20.4 44.1 %copy-start.19 = (s32[512,1]{0,1:T(1,128)}, s32[512,1]{0,1:T(1,128)S(1)}, u32[]{:S(2)}) copy-start(s32[512,1]{0,1:T(1,128)S(1)} %compare_select_fusion.1) | copy-start | bytes 6148
  20.4 35.3 %copy-start.20 = (bf16[4,8]{1,0:T(4,128)(2,1)}, bf16[4,8]{1,0:T(4,128)(2,1)S(1)}, u32[]{:S(2)}) copy-start(bf16[4,8]{1,0:T(4,128)(2,1)S(1)} %get-tuple-element.32) | copy-start | bytes 196
  21.5 0.8 slice-start
  22.5 41.9 %copy-start.11 = (pred[512]{0:T(512)(128)(4,1)}, pred[512]{0:T(512)(128)(4,1)S(1)}, u32[]{:S(2)}) copy-start(pred[512]{0:T(512)(128)(4,1)S(1)} %lt.98) | copy-start | bytes 1540
  27.8 5.1 %copy-start.6 = (bf16[2,64,512]{2,1,0:T(8,128)(2,1)S(1)}, bf16[2,64,512]{2,1,0:T(8,128)(2,1)}, u32[]{:S(2)}) copy-start(bf16[2,64,512]{2,1,0:T(8,128)(2,1)} %param.8) | copy-start | bytes 393220
  27.8 5.1 %copy-start.1 = (bf16[2,64,512]{2,1,0:T(8,128)(2,1)S(1)}, bf16[2,64,512]{2,1,0:T(8,128)(2,1)}, u32[]{:S(2)}) copy-start(bf16[2,64,512]{2,1,0:T(8,128)(2,1)} %param.9) | copy-start | bytes 393220
  40.7 10.4 %all-to-all-start.2 = ((bf16[16,2,1024]{2,1,0:T(2,128)(2,1)}), bf16[16,2,1024]{2,1,0:T(2,128)(2,1)S(1)}, u32[]{:S(2)}, u32[]{:S(2)}) async-start(bf16[16,2,1024]{2,1,0:T(2,128)(2,1)} %reshape.448), calls=%async_computation.2 | async-start | bytes 131072 | tf_op jit(solution)/shard_map/all_to_all | solution.py:23
  51.1 11.7 %all-to-all-start.1 = ((f32[16,1,2048]{2,1,0:T(1,128)}), f32[16,1,2048]{2,1,0:T(1,128)S(1)}, u32[]{:S(2)}, u32[]{:S(2)}) async-start(f32[16,1,2048]{2,1,0:T(1,128)} %reshape.446), calls=%async_computation.1 | async-start | bytes 262144 | tf_op jit(solution)/shard_map/all_to_all | solution.py:53
  68.0 0.8 copy-start.5
  68.0 0.9 copy-start.7
  76.7 11.3 %all-to-all-start.4 = ((bf16[16,2,1024]{2,1,0:T(2,128)(2,1)}), bf16[16,2,1024]{2,1,0:T(2,128)(2,1)S(1)}, u32[]{:S(2)}, u32[]{:S(2)}) async-start(bf16[16,2,1024]{2,1,0:T(2,128)(2,1)} %reshape.452), calls=%async_computation.4 | async-start | bytes 131072 | tf_op jit(solution)/shard_map/all_to_all | solution.py:23
  88.0 12.3 %all-to-all-start.3 = ((f32[16,1,2048]{2,1,0:T(1,128)}), f32[16,1,2048]{2,1,0:T(1,128)S(1)}, u32[]{:S(2)}, u32[]{:S(2)}) async-start(f32[16,1,2048]{2,1,0:T(1,128)} %reshape.450), calls=%async_computation.3 | async-start | bytes 262144 | tf_op jit(solution)/shard_map/all_to_all | solution.py:53
  114.2 11.9 %all-to-all-start.6 = ((bf16[16,2,1024]{2,1,0:T(2,128)(2,1)}), bf16[16,2,1024]{2,1,0:T(2,128)(2,1)S(1)}, u32[]{:S(2)}, u32[]{:S(2)}) async-start(bf16[16,2,1024]{2,1,0:T(2,128)(2,1)} %reshape.456), calls=%async_computation.6 | async-start | bytes 131072 | tf_op jit(solution)/shard_map/all_to_all | solution.py:23
  126.1 12.3 %all-to-all-start.5 = ((f32[16,1,2048]{2,1,0:T(1,128)}), f32[16,1,2048]{2,1,0:T(1,128)S(1)}, u32[]{:S(2)}, u32[]{:S(2)}) async-start(f32[16,1,2048]{2,1,0:T(1,128)} %reshape.454), calls=%async_computation.5 | async-start | bytes 262144 | tf_op jit(solution)/shard_map/all_to_all | solution.py:53
  130.4 110.0 %all-reduce.3.cloned.1.call-start = ((), (), s32[]{:S(2)}) async-start(), calls=%async_computation.8 | async-start | bytes 262144 | tf_op jit(solution)/shard_map/psum | solution.py:121
  153.9 88.1 %all-to-all-start.7 = ((f32[16,1,2048]{2,1,0:T(1,128)}), f32[16,1,2048]{2,1,0:T(1,128)S(1)}, u32[]{:S(2)}, u32[]{:S(2)}) async-start(f32[16,1,2048]{2,1,0:T(1,128)} %reshape.458), calls=%async_computation.7 | async-start | bytes 262144 | tf_op jit(solution)/shard_map/all_to_all | solution.py:53
  240.5 0.8 copy-start.9
  240.5 0.8 copy-start.10
  (8 other events, 5.5 us)
Sparse Core Ops, SparseCore 0:
  153.2 87.2 all-reduce.2
where the time goes:
time: 257 us; the launch traced here: 254 us
  waiting for transfers between devices  95.5 us (37%)
  blocking collectives  40.2 us (16%)
  starting transfers between devices  37.2 us (14%)
  other arithmetic  30 us (12%)
  local copies, waits for them, and re-layouts  28.2 us (11%)
  between operations  15.1 us (6%)
  matrix products  8.26 us (3%)
    psum x1, waiting for transfers between devices, on_device(): weight_one, weight_two = lax.psum((weight_one, weight_two), ('dom', 'sub'))  82.2 us
    all_gather x4, blocking collectives, mix_forward(): lax.all_gather(message, 'chan', axis=0, tiled=True)  20.4 us
    all_to_all x4, starting transfers between devices, send_halo(): lax.all_to_all(outgoing, ('dom', 'sub'), split_axis=1, concat_axis=1, til...  20.3 us
    all_gather x4, blocking collectives, mix_backward(): lax.all_gather(slope, 'chan', axis=0, tiled=True)  19.8 us
    all_to_all x4, starting transfers between devices, propagate_back(): lax.all_to_all(outgoing, ('dom', 'sub'), split_axis=1, concat_axis=1, til...  16.8 us
    unnamed x63, local copies, waits for them, and re-layouts  14.4 us
    scatter-add x4, other arithmetic, propagate_back(): local_part.at[:, send_rows[0].reshape(-1)]  14.1 us
    all_to_all x4, waiting for transfers between devices, send_halo(): lax.all_to_all(outgoing, ('dom', 'sub'), split_axis=1, concat_axis=1, til...  9.52 us
  transfers between devices with their start and end apart: 9, of which 8 were waited for; matrix products, arithmetic and copies ran while one was open for 8% of the time, Pallas kernels for 0%

commit v1 on v0

v1 whole, which is shorter than its diff:
```python
import functools
import math

import jax
import jax.numpy as jnp
from jax import lax
from jax.experimental import pallas as pl
from jax.experimental.pallas import tpu as pltpu
from jax.sharding import PartitionSpec as P

MESH = pl.DeviceIdType.MESH
F32 = jnp.float32
BF16 = jnp.bfloat16


def sigmoid(value):
    return 1.0 / (1.0 + jnp.exp(-value))


def dot(a, b):
    return jnp.dot(a, b, preferred_element_type=F32)


def dot_nt(a, b):
    return lax.dot_general(a, b, (((1,), (1,)), ((), ())), preferred_element_type=F32)


def dot_tn(a, b):
    return lax.dot_general(a, b, (((0,), (0,)), ((), ())), preferred_element_type=F32)


def kernel(
    blocks, subs, chans, slots_each, rows_each, factor,
    y_ref, dy_ref, weights_ref, tiles_ref, cols_ref, mask_ref, slot_ref,
    grads_ref, wgrads_ref,
    full, gather, scatter, pick, put, ext, out, back, ret, wpart, wsum, wred, wall, square, wide, held, msgs, slopes,
    chan_send, chan_recv, send_sem, recv_sem,
):
    layers = weights_ref.shape[0]
    _, part, rows = y_ref.shape
    channels = part * chans
    row_blocks, tile_slots = cols_ref.shape
    tile = tiles_ref.shape[-1]
    col_blocks = ext.shape[1] // tile
    my_sub = lax.axis_index("sub")
    me = lax.axis_index("dom") * subs + my_sub
    my_chan = lax.axis_index("chan")

    def block_of(step):
        peer = lax.rem(me + step, blocks)
        return peer, {"dom": peer // subs, "sub": lax.rem(peer, subs)}

    def chan_of(step):
        return {"chan": lax.rem(my_chan + step, chans)}

    barrier = pltpu.get_barrier_semaphore()

    @pl.loop(1, blocks)
    def _(step):
        pl.semaphore_signal(barrier, inc=1, device_id=block_of(step)[1], device_id_type=MESH)

    for step in range(1, chans):
        pl.semaphore_signal(barrier, inc=1, device_id=chan_of(step), device_id_type=MESH)
    pl.semaphore_wait(barrier, blocks - 1 + chans - 1)

    mine = pl.ds(pl.multiple_of(my_chan * part, part), part)

    def chan_copy(field, step):
        source = y_ref.at[field] if field < 2 else dy_ref.at[field - 2]
        return pltpu.make_async_remote_copy(
            src_ref=source,
            dst_ref=full.at[field, mine],
            send_sem=chan_send.at[field, step],
            recv_sem=chan_recv.at[field, step],
            device_id=chan_of(step),
            device_id_type=MESH,
        )

    order = (0, 1, 3, 2)
    for field in order:
        for step in range(1, chans):
            chan_copy(field, step).start()

    def copy_of(index, source, target, offset, size, spread):
        def one(step):
            peer, device = block_of(step)
            src = source.at[pl.ds(pl.multiple_of(peer * size, size), size)] if spread else source
            return pltpu.make_async_remote_copy(
                src_ref=src,
                dst_ref=target.at[pl.ds(pl.multiple_of(offset + me * size, size), size)],
                send_sem=send_sem.at[index, step],
                recv_sem=recv_sem.at[index, step],
                device_id=device,
                device_id_type=MESH,
            )

        return one

    def start(one):
        @pl.loop(1, blocks)
        def _(step):
            one(step).start()

    def finish(one):
        @pl.loop(1, blocks)
        def _(step):
            one(step).wait()

    own_slots = pl.ds(pl.multiple_of(me * slots_each, slots_each), slots_each)
    own_extended = pl.ds(pl.multiple_of(rows + me * slots_each, slots_each), slots_each)
    blank = jnp.zeros((slots_each, channels), BF16)
    for index in range(2 * layers):
        ext[index, own_extended, :] = blank
        ret[index, own_slots, :] = blank

    halo = blocks * slots_each
    slot_row = slot_ref[...]
    put[...] = (lax.broadcasted_iota(jnp.int32, (rows, halo), 0) == slot_row).astype(F32).astype(BF16)
    for at in range(0, halo, tile):
        column = jnp.broadcast_to(slot_row[:, at : at + tile].astype(F32), (tile, tile)).T
        for row_at in range(0, rows, tile):
            lanes = (lax.broadcasted_iota(jnp.int32, (tile, tile), 1) + row_at).astype(F32)
            pick[at : at + tile, row_at : row_at + tile] = (lanes == column).astype(F32).astype(BF16)

    for row_block in range(row_blocks):
        row_span = slice(row_block * tile, (row_block + 1) * tile)

        def place(col, carry):
            slot = jnp.int32(0)
            live = jnp.int32(0)
            for k in range(tile_slots):
                hit = (cols_ref[row_block, k] == col) & (mask_ref[row_block, k] > 0)
                slot = jnp.where(hit, k, slot)
                live = jnp.where(hit, 1, live)
            block = tiles_ref[row_block, slot].astype(F32) * live.astype(F32)
            span = pl.ds(pl.multiple_of(col * tile, tile), tile)
            scatter[span, row_span] = block.astype(BF16)
            gather[row_span, span] = block.T.astype(BF16)
            return carry

        lax.fori_loop(0, col_blocks, place, 0)

    def arrived(field):
        for step in range(1, chans):
            chan_copy(field, step).wait()
        source = y_ref[field] if field < 2 else dy_ref[field - 2]
        full[field, mine, :] = source
        return full[field].astype(F32).T

    def forward(index):
        return copy_of(index, out.at[index], ext.at[index], rows, slots_each, True)

    def backward(index):
        return copy_of(2 * layers + index, back.at[index], ret.at[index], 0, slots_each, True)

    def send_field(index, field):
        out[index] = dot(pick[...], field).astype(BF16)
        start(forward(index))
        return dot(gather[:, :rows], field)

    def message(index, own):
        finish(forward(index))
        return (own + dot(gather[:, rows:], ext[index, rows:, :])).astype(BF16)

    def send_gradient(index, field):
        back[index] = dot(scatter[rows:, :], field).astype(BF16)
        start(backward(index))
        return dot(scatter[:rows, :], field)

    def returned(index):
        finish(backward(index))
        return dot(put[...], ret[index])

    def weight_part(layer, which, moved, slope):
        square[...] = dot_tn(moved, slope)
        at = (layer * 2 + which) * part
        wpart[at : at + part, :] = square[mine, :]

    used = 2 * layers * part
    if used < wpart.shape[0]:
        wpart[used:, :] = jnp.zeros((wpart.shape[0] - used, channels), F32)

    held[0] = arrived(0)
    held[4] = send_field(0, held[0].astype(BF16))
    held[1] = arrived(1)
    held[3] = arrived(3)
    held[2] = arrived(2)
    moves = 0
    pending = None
    for layer in reversed(range(layers)):
        first = weights_ref[layer, 0]
        second = weights_ref[layer, 1]
        msgs[1] = message(moves, held[4])
        linear_two = dot(msgs[1], second)
        gate_two = sigmoid(linear_two)
        held[5] = gate_two * (1.0 + linear_two * (1.0 - gate_two))
        input_two = (held[1] - linear_two * gate_two).astype(BF16)
        held[1] = input_two.astype(F32)
        held[4] = send_field(moves + 1, input_two)
        if pending is not None:
            held[3] += returned(pending)
        slopes[1] = (held[3] * held[5]).astype(BF16)
        held[2] += send_gradient(moves, dot_nt(slopes[1], second).astype(BF16))
        weight_part(layer, 1, msgs[1], slopes[1])
        msgs[0] = message(moves + 1, held[4])
        linear_one = dot(msgs[0], first)
        gate_one = sigmoid(linear_one)
        held[5] = gate_one * (1.0 + linear_one * (1.0 - gate_one))
        if layer > 0:
            state_one = (held[0] - linear_one * gate_one).astype(BF16)
            held[0] = state_one.astype(F32)
            held[4] = send_field(moves + 2, state_one)
        held[2] += returned(moves)
        slopes[0] = (held[2] * held[5]).astype(BF16)
        held[3] += send_gradient(moves + 1, dot_nt(slopes[0], first).astype(BF16))
        weight_part(layer, 0, msgs[0], slopes[0])
        pending = moves + 1
        moves += 2

    reduce_copy = copy_of(4 * layers, wpart, wsum, 0, rows_each, True)
    start(reduce_copy)
    own_piece = pl.ds(pl.multiple_of(me * rows_each, rows_each), rows_each)
    wsum[own_piece, :] = wpart[own_piece, :]
    wide[...] = held[2].T
    grads_ref[0] = wide[mine, :].astype(BF16)
    finish(reduce_copy)
    total = wsum[:rows_each, :]
    for piece in range(1, blocks):
        total = total + wsum[piece * rows_each : (piece + 1) * rows_each, :]
    wred[...] = total * factor
    spread_copy = copy_of(4 * layers + 1, wred, wall, 0, rows_each, False)
    start(spread_copy)
    wall[own_piece, :] = wred[...]
    wide[...] = (held[3] + returned(pending)).T
    grads_ref[1] = wide[mine, :].astype(BF16)
    finish(spread_copy)
    for layer in range(layers):
        for which in range(2):
            at = (layer * 2 + which) * part
            wgrads_ref[layer, which] = wall[at : at + part, :]


def solution(mesh):
    blocks = mesh.shape["dom"] * mesh.shape["sub"]
    subs = mesh.shape["sub"]
    chans = mesh.shape["chan"]

    def on_device(y_last, dy_last, weights, tile_vals, tile_cols, tile_mask, send_rows, send_count):
        _, part, rows = y_last.shape
        layers = weights.shape[0]
        channels = part * chans
        slots_each = send_rows.shape[2]
        halo = blocks * slots_each
        live = jnp.arange(slots_each, dtype=jnp.int32)[None, :] < send_count[0][:, None]
        slot_row = jnp.where(live, send_rows[0], -1).reshape(1, halo)
        rows_each = max(8, 2 * layers * part // blocks)
        pieces = blocks * rows_each
        exchanges = 4 * layers + 2
        factor = 1.0 / math.sqrt(rows * blocks)
        vmem = pl.BlockSpec(memory_space=pltpu.VMEM)
        smem = pl.BlockSpec(memory_space=pltpu.SMEM)
        return pl.pallas_call(
            functools.partial(kernel, blocks, subs, chans, slots_each, rows_each, factor),
            out_shape=(
                jax.ShapeDtypeStruct(y_last.shape, BF16),
                jax.ShapeDtypeStruct((layers, 2, part, channels), F32),
            ),
            in_specs=[vmem, vmem, vmem, vmem, smem, smem, vmem],
            out_specs=(vmem, vmem),
            scratch_shapes=[
                pltpu.VMEM((4, channels, rows), BF16),
                pltpu.VMEM((rows, rows + halo), BF16),
                pltpu.VMEM((rows + halo, rows), BF16),
                pltpu.VMEM((halo, rows), BF16),
                pltpu.VMEM((rows, halo), BF16),
                pltpu.VMEM((2 * layers, rows + halo, channels), BF16),
                pltpu.VMEM((2 * layers, halo, channels), BF16),
                pltpu.VMEM((2 * layers, halo, channels), BF16),
                pltpu.VMEM((2 * layers, halo, channels), BF16),
                pltpu.VMEM((pieces, channels), F32),
                pltpu.VMEM((pieces, channels), F32),
                pltpu.VMEM((rows_each, channels), F32),
                pltpu.VMEM((pieces, channels), F32),
                pltpu.VMEM((channels, channels), F32),
                pltpu.VMEM((channels, rows), F32),
                pltpu.VMEM((6, rows, channels), F32),
                pltpu.VMEM((2, rows, channels), BF16),
                pltpu.VMEM((2, rows, channels), BF16),
                pltpu.SemaphoreType.DMA((4, chans)),
                pltpu.SemaphoreType.DMA((4, chans)),
                pltpu.SemaphoreType.DMA((exchanges, blocks)),
                pltpu.SemaphoreType.DMA((exchanges, blocks)),
            ],
            compiler_params=pltpu.CompilerParams(
                collective_id=0, has_side_effects=True, vmem_limit_bytes=44 * 1024 * 1024
            ),
        )(y_last, dy_last, weights, tile_vals, tile_cols, tile_mask, slot_row)

    return jax.shard_map(
        on_device,
        mesh=mesh,
        in_specs=(
            P(None, "chan", ("groups", "dom", "sub")),
            P(None, "chan", ("groups", "dom", "sub")),
            P(),
            P(("groups", "dom", "sub"), None, None, None),
            P(("groups", "dom", "sub"), None),
            P(("groups", "dom", "sub"), None),
            P(("groups", "dom", "sub"), None, None),
            P(("groups", "dom", "sub"), None),
        ),
        out_specs=(P(None, "chan", ("groups", "dom", "sub")), P("groups", None, "chan", None)),
        check_vma=False,
    )
```

time: 257 us -> 62.6 us (0.24)
  waiting for transfers between devices: 95.5 us -> 0 us
  Pallas kernels: 0 us -> 54.7 us
  blocking collectives: 40.2 us -> 0 us
  starting transfers between devices: 37.2 us -> 0 us
  other arithmetic: 30 us -> 0.08 us
  local copies, waits for them, and re-layouts: 28.2 us -> 6.81 us
  between operations: 15.1 us -> 0.66 us
  matrix products: 8.26 us -> 0 us
    psum x1 -> x0, waiting for transfers between devices: 82.2 us -> none  [on_device(): weight_one, weight_two = lax.psum((weight_one, weight_two), ('dom', 'sub'))]
    pallas_call x0 -> x1, Pallas kernels: none -> 54.7 us  [on_device(): pl.pallas_call(functools.partial(kernel, blocks, subs, chans, slots_each,...]
    all_gather x8 -> x0, blocking collectives: 40.2 us -> none  [the longest x4 20.4 us: mix_forward(): lax.all_gather(message, 'chan', axis=0, tiled=True)]
    all_to_all x8 -> x0, starting transfers between devices: 37.2 us -> none  [the longest x4 20.3 us: send_halo(): lax.all_to_all(outgoing, ('dom', 'sub'), split_axis=1, concat_axis=1, til...]
    scatter-add x8 -> x0, other arithmetic: 22.6 us -> none  [the longest x4 14.1 us: propagate_back(): local_part.at[:, send_rows[0].reshape(-1)]]
    all_to_all x8 -> x0, waiting for transfers between devices: 13.4 us -> none  [the longest x4 9.52 us: send_halo(): lax.all_to_all(outgoing, ('dom', 'sub'), split_axis=1, concat_axis=1, til...]
    unnamed x63 -> x16, local copies, waits for them, and re-layouts: 14.4 us -> 5.94 us
    dot_general x20 -> x0, matrix products: 8.26 us -> none  [the longest x4 3.12 us: accumulate(): jnp.einsum('ir,or->io', message, incoming, preferred_element_type=jnp.flo...]
  transfers between devices with their start and end apart: 9 -> 0, of which waited for: 8 -> 0; matrix products, arithmetic and copies ran while one was open for 8% -> 0% of each run, Pallas kernels for 0% -> 0%
where the time goes in v1:
time: 62.6 us; the launch traced here: 62.3 us
  Pallas kernels  54.7 us (87%)
  local copies, waits for them, and re-layouts  6.81 us (11%)
  between operations  0.66 us (1%)
    pallas_call x1, Pallas kernels, on_device(): pl.pallas_call(functools.partial(kernel, blocks, subs, chans, slots_each,...  54.7 us
    unnamed x16, local copies, waits for them, and re-layouts  5.94 us

profile of v1, /device:TPU:0, one launch (start us, length us, event | category | flops | bytes accessed | tf_op | source)
XLA Modules:
  0.0 62.3 jit_solution(5051656306231627383)
XLA Ops:
  0.6 0.0 copy-start.6
  0.6 0.8 %squeeze.3 = s32[1,512]{1,0:T(1,128)S(1)} reshape(s32[1,16,32]{2,1,0:T(8,128)} %param.14) | data formatting | bytes 4096 | tf_op jit(solution)/shard_map/squeeze | solution.py:255
  1.4 0.0 copy-done.6
  1.4 0.1 iota_compare_fusion
  1.5 0.1 lt.29
  1.6 0.0 copy-start.4
  1.6 0.0 copy-start.5
  1.6 0.7 %copy-done.4 = s32[4,8]{1,0:T(4,128)S(1)} copy-done((s32[4,8]{1,0:T(4,128)S(1)}, s32[4,8]{1,0:T(4,128)}, u32[]{:S(2)}) %copy-start.4) | copy-done | bytes 152
  2.3 0.0 copy-done.5
  2.3 0.0 copy-start
  2.3 1.2 %copy-done = bf16[4,8,128,128]{3,2,1,0:T(8,128)(2,1)S(1)} copy-done((bf16[4,8,128,128]{3,2,1,0:T(8,128)(2,1)S(1)}, bf16[4,8,128,128]{3,2,1,0:T(8,128)(2,1)}, u32[]{:S(2)}) %copy-start) | copy-done | bytes 1048600
  3.5 0.0 copy-start.1
  3.5 0.9 %copy-done.1 = bf16[2,64,512]{2,1,0:T(8,128)(2,1)S(1)} copy-done((bf16[2,64,512]{2,1,0:T(8,128)(2,1)S(1)}, bf16[2,64,512]{2,1,0:T(8,128)(2,1)}, u32[]{:S(2)}) %copy-start.1) | copy-done | bytes 131096
  4.4 0.0 copy-start.2
  4.4 0.9 %copy-done.2 = bf16[2,64,512]{2,1,0:T(8,128)(2,1)S(1)} copy-done((bf16[2,64,512]{2,1,0:T(8,128)(2,1)S(1)}, bf16[2,64,512]{2,1,0:T(8,128)(2,1)}, u32[]{:S(2)}) %copy-start.2) | copy-done | bytes 131096
  5.3 0.0 copy-start.3
  5.3 0.9 %copy-done.3 = bf16[2,2,128,128]{3,2,1,0:T(8,128)(2,1)S(1)} copy-done((bf16[2,2,128,128]{3,2,1,0:T(8,128)(2,1)S(1)}, bf16[2,2,128,128]{3,2,1,0:T(8,128)(2,1)}, u32[]{:S(2)}) %copy-start.3) | copy-done | bytes 131096
  6.2 54.7 %shard_map.95 = (bf16[2,64,512]{2,1,0:T(8,128)(2,1)S(1)}, f32[2,2,64,128]{3,2,1,0:T(8,128)S(1)}) custom-call(bf16[2,64,512]{2,1,0:T(8,128)(2,1)S(1)} %copy-done.1, bf16[2,64,512]{2,1,0:T(8,128)(2,1)S(1)} %copy-done.2, bf16[2,2,128,128]{3,2,1,0:T(8,128)(2,1)S(1)} %copy-done.3, bf16[4,8,128,128]{3,2,1,0:T(8,128)(2,1)S(1)} %copy-done, s32[4,8]{1,0:T(4,128)S(1)} %copy-done.4, ...), custom_call_target="tpu_custom_call" | custom-call | tf_op jit(solution)/shard_map/pallas_call | solution.py:262
  61.0 0.7 %copy.12 = bf16[2,64,512]{2,1,0:T(8,128)(2,1)} copy(bf16[2,64,512]{2,1,0:T(8,128)(2,1)S(1)} %get-tuple-element.4) | data formatting | bytes 262144
  61.6 0.7 %copy.13 = f32[2,2,64,128]{3,2,1,0:T(8,128)} copy(f32[2,2,64,128]{3,2,1,0:T(8,128)S(1)} %get-tuple-element.5) | data formatting | bytes 262144
  (1 shorter events, 0.0 us)
Async XLA Ops:
  0.6 0.8 %copy-start.6 = (s32[1,16]{1,0:T(1,128)S(1)}, s32[1,16]{1,0:T(1,128)}, u32[]{:S(2)}) copy-start(s32[1,16]{1,0:T(1,128)} %param.15) | copy-start | bytes 196
  1.6 0.7 %copy-start.4 = (s32[4,8]{1,0:T(4,128)S(1)}, s32[4,8]{1,0:T(4,128)}, u32[]{:S(2)}) copy-start(s32[4,8]{1,0:T(4,128)} %cols_ref.1) | copy-start | bytes 388
  1.6 0.7 %copy-start.5 = (s32[4,8]{1,0:T(4,128)S(1)}, s32[4,8]{1,0:T(4,128)}, u32[]{:S(2)}) copy-start(s32[4,8]{1,0:T(4,128)} %mask_ref.1) | copy-start | bytes 388
  2.3 1.2 %copy-start = (bf16[4,8,128,128]{3,2,1,0:T(8,128)(2,1)S(1)}, bf16[4,8,128,128]{3,2,1,0:T(8,128)(2,1)}, u32[]{:S(2)}) copy-start(bf16[4,8,128,128]{3,2,1,0:T(8,128)(2,1)} %tiles_ref.1) | copy-start | bytes 3145732
  3.5 0.9 %copy-start.1 = (bf16[2,64,512]{2,1,0:T(8,128)(2,1)S(1)}, bf16[2,64,512]{2,1,0:T(8,128)(2,1)}, u32[]{:S(2)}) copy-start(bf16[2,64,512]{2,1,0:T(8,128)(2,1)} %y_ref.1) | copy-start | bytes 393220
  4.4 0.9 %copy-start.2 = (bf16[2,64,512]{2,1,0:T(8,128)(2,1)S(1)}, bf16[2,64,512]{2,1,0:T(8,128)(2,1)}, u32[]{:S(2)}) copy-start(bf16[2,64,512]{2,1,0:T(8,128)(2,1)} %dy_ref.1) | copy-start | bytes 393220
  5.3 0.9 %copy-start.3 = (bf16[2,2,128,128]{3,2,1,0:T(8,128)(2,1)S(1)}, bf16[2,2,128,128]{3,2,1,0:T(8,128)(2,1)}, u32[]{:S(2)}) copy-start(bf16[2,2,128,128]{3,2,1,0:T(8,128)(2,1)} %weights_ref.1) | copy-start | bytes 393220

commit v2 on v1

--- a/solution.py
+++ b/solution.py
@@ -31,13 +31,13 @@
 
 def kernel(
     blocks, subs, chans, slots_each, rows_each, factor,
-    y_ref, dy_ref, weights_ref, tiles_ref, cols_ref, mask_ref, slot_ref,
+    y_hbm, dy_hbm, weights_hbm, tiles_hbm, cols_ref, mask_ref, rows_hbm, count_hbm,
     grads_ref, wgrads_ref,
     full, gather, scatter, pick, put, ext, out, back, ret, wpart, wsum, wred, wall, square, wide, held, msgs, slopes,
-    chan_send, chan_recv, send_sem, recv_sem,
+    weights_ref, tiles_ref, rows_ref, count_ref, chan_send, chan_recv, send_sem, recv_sem, local_sem,
 ):
     layers = weights_ref.shape[0]
-    _, part, rows = y_ref.shape
+    _, part, rows = y_hbm.shape
     channels = part * chans
     row_blocks, tile_slots = cols_ref.shape
     tile = tiles_ref.shape[-1]
@@ -53,6 +53,22 @@
     def chan_of(step):
         return {"chan": lax.rem(my_chan + step, chans)}
 
+    mine = pl.ds(pl.multiple_of(my_chan * part, part), part)
+
+    def source_of(field):
+        return y_hbm.at[field] if field < 2 else dy_hbm.at[field - 2]
+
+    rows_in = pltpu.make_async_copy(rows_hbm, rows_ref, local_sem.at[0])
+    count_in = pltpu.make_async_copy(count_hbm, count_ref, local_sem.at[1])
+    tiles_in = pltpu.make_async_copy(tiles_hbm, tiles_ref, local_sem.at[2])
+    weights_in = pltpu.make_async_copy(weights_hbm, weights_ref, local_sem.at[3])
+    fields_in = [
+        pltpu.make_async_copy(source_of(field), full.at[field, mine], local_sem.at[4 + field])
+        for field in range(4)
+    ]
+    for copy in (rows_in, count_in, *fields_in, tiles_in, weights_in):
+        copy.start()
+
     barrier = pltpu.get_barrier_semaphore()
 
     @pl.loop(1, blocks)
@@ -63,12 +79,9 @@
         pl.semaphore_signal(barrier, inc=1, device_id=chan_of(step), device_id_type=MESH)
     pl.semaphore_wait(barrier, blocks - 1 + chans - 1)
 
-    mine = pl.ds(pl.multiple_of(my_chan * part, part), part)
-
     def chan_copy(field, step):
-        source = y_ref.at[field] if field < 2 else dy_ref.at[field - 2]
         return pltpu.make_async_remote_copy(
-            src_ref=source,
+            src_ref=source_of(field),
             dst_ref=full.at[field, mine],
             send_sem=chan_send.at[field, step],
             recv_sem=chan_recv.at[field, step],
@@ -97,12 +110,12 @@
         return one
 
     def start(one):
-        @pl.loop(1, blocks)
+        @pl.loop(1, blocks, unroll=3)
         def _(step):
             one(step).start()
 
     def finish(one):
-        @pl.loop(1, blocks)
+        @pl.loop(1, blocks, unroll=3)
         def _(step):
             one(step).wait()
 
@@ -114,14 +127,72 @@
         ret[index, own_slots, :] = blank
 
     halo = blocks * slots_each
-    slot_row = slot_ref[...]
-    put[...] = (lax.broadcasted_iota(jnp.int32, (rows, halo), 0) == slot_row).astype(F32).astype(BF16)
+    rows_in.wait()
+    count_in.wait()
+    slot_at = lax.broadcasted_iota(jnp.int32, (blocks, halo), 1)
+    block_at = lax.broadcasted_iota(jnp.int32, (blocks, halo), 0)
+    offset = slot_at - block_at * slots_each
+    inside = (offset >= 0) & (offset < slots_each)
+    within = jnp.sum(jnp.where(inside, offset, 0).astype(F32), axis=0, keepdims=True)
+    spread = inside.astype(F32).astype(BF16)
+    entry = lax.broadcasted_iota(jnp.int32, (slots_each, halo), 0).astype(F32)
+    matching = (entry == within).astype(F32).astype(BF16)
+    listed = rows_ref[0]
+    high = dot((listed >> 8).astype(F32).astype(BF16), matching)
+    low = dot((listed & 255).astype(F32).astype(BF16), matching)
+    chosen = jnp.sum(jnp.where(inside, high * 256.0 + low, 0.0), axis=0, keepdims=True)
+    counts = jnp.broadcast_to(count_ref[...].astype(F32), (8, blocks)).astype(BF16)
+    limit = dot(counts, spread)[0:1]
+    slot_row = jnp.where(within < limit, chosen, -1.0)
     for at in range(0, halo, tile):
-        column = jnp.broadcast_to(slot_row[:, at : at + tile].astype(F32), (tile, tile)).T
+        column = jnp.broadcast_to(slot_row[:, at : at + tile], (tile, tile)).T
         for row_at in range(0, rows, tile):
             lanes = (lax.broadcasted_iota(jnp.int32, (tile, tile), 1) + row_at).astype(F32)
             pick[at : at + tile, row_at : row_at + tile] = (lanes == column).astype(F32).astype(BF16)
 
+    def arrived(field):
+        for step in range(1, chans):
+            chan_copy(field, step).wait()
+        fields_in[field].wait()
+        return full[field].astype(F32).T
+
+    def forward(index):
+        return copy_of(index, out.at[index], ext.at[index], rows, slots_each, True)
+
+    def backward(index):
+        return copy_of(2 * layers + index, back.at[index], ret.at[index], 0, slots_each, True)
+
+    def send_field(index, field):
+        out[index] = dot(pick[...], field).astype(BF16)
+        start(forward(index))
+        return dot(gather[:, :rows], field)
+
+    def message(index, own):
+        finish(forward(index))
+        return (own + dot(gather[:, rows:], ext[index, rows:, :])).astype(BF16)
+
+    def send_gradient(index, field):
+        back[index] = dot(scatter[rows:, :], field).astype(BF16)
+        start(backward(index))
+        return dot(scatter[:rows, :], field)
+
+    def returned(index):
+        finish(backward(index))
+        return dot(put[...], ret[index])
+
+    def weight_part(layer, which, moved, slope):
+        square[...] = dot_tn(moved, slope)
+        at = (layer * 2 + which) * part
+        wpart[at : at + part, :] = square[mine, :]
+
+    used = 2 * layers * part
+    if used < wpart.shape[0]:
+        wpart[used:, :] = jnp.zeros((wpart.shape[0] - used, channels), F32)
+
+    held[0] = arrived(0)
+    out[0] = dot(pick[...], held[0].astype(BF16)).astype(BF16)
+    start(forward(0))
+    tiles_in.wait()
     for row_block in range(row_blocks):
         row_span = slice(row_block * tile, (row_block + 1) * tile)
 
@@ -140,51 +211,12 @@
 
         lax.fori_loop(0, col_blocks, place, 0)
 
-    def arrived(field):
-        for step in range(1, chans):
-            chan_copy(field, step).wait()
-        source = y_ref[field] if field < 2 else dy_ref[field - 2]
-        full[field, mine, :] = source
-        return full[field].astype(F32).T
-
-    def forward(index):
-        return copy_of(index, out.at[index], ext.at[index], rows, slots_each, True)
-
-    def backward(index):
-        return copy_of(2 * layers + index, back.at[index], ret.at[index], 0, slots_each, True)
-
-    def send_field(index, field):
-        out[index] = dot(pick[...], field).astype(BF16)
-        start(forward(index))
-        return dot(gather[:, :rows], field)
-
-    def message(index, own):
-        finish(forward(index))
-        return (own + dot(gather[:, rows:], ext[index, rows:, :])).astype(BF16)
-
-    def send_gradient(index, field):
-        back[index] = dot(scatter[rows:, :], field).astype(BF16)
-        start(backward(index))
-        return dot(scatter[:rows, :], field)
-
-    def returned(index):
-        finish(backward(index))
-        return dot(put[...], ret[index])
-
-    def weight_part(layer, which, moved, slope):
-        square[...] = dot_tn(moved, slope)
-        at = (layer * 2 + which) * part
-        wpart[at : at + part, :] = square[mine, :]
-
-    used = 2 * layers * part
-    if used < wpart.shape[0]:
-        wpart[used:, :] = jnp.zeros((wpart.shape[0] - used, channels), F32)
-
-    held[0] = arrived(0)
-    held[4] = send_field(0, held[0].astype(BF16))
+    held[4] = dot(gather[:, :rows], held[0].astype(BF16))
+    put[...] = (lax.broadcasted_iota(jnp.int32, (rows, halo), 0).astype(F32) == slot_row).astype(F32).astype(BF16)
     held[1] = arrived(1)
     held[3] = arrived(3)
     held[2] = arrived(2)
+    weights_in.wait()
     moves = 0
     pending = None
     for layer in reversed(range(layers)):
@@ -251,13 +283,12 @@
         channels = part * chans
         slots_each = send_rows.shape[2]
         halo = blocks * slots_each
-        live = jnp.arange(slots_each, dtype=jnp.int32)[None, :] < send_count[0][:, None]
-        slot_row = jnp.where(live, send_rows[0], -1).reshape(1, halo)
         rows_each = max(8, 2 * layers * part // blocks)
         pieces = blocks * rows_each
         exchanges = 4 * layers + 2
         factor = 1.0 / math.sqrt(rows * blocks)
         vmem = pl.BlockSpec(memory_space=pltpu.VMEM)
+        hbm = pl.BlockSpec(memory_space=pl.ANY)
         smem = pl.BlockSpec(memory_space=pltpu.SMEM)
         return pl.pallas_call(
             functools.partial(kernel, blocks, subs, chans, slots_each, rows_each, factor),
@@ -265,7 +296,7 @@
                 jax.ShapeDtypeStruct(y_last.shape, BF16),
                 jax.ShapeDtypeStruct((layers, 2, part, channels), F32),
             ),
-            in_specs=[vmem, vmem, vmem, vmem, smem, smem, vmem],
+            in_specs=[hbm, hbm, hbm, hbm, smem, smem, hbm, hbm],
             out_specs=(vmem, vmem),
             scratch_shapes=[
                 pltpu.VMEM((4, channels, rows), BF16),
@@ -286,15 +317,20 @@
                 pltpu.VMEM((6, rows, channels), F32),
                 pltpu.VMEM((2, rows, channels), BF16),
                 pltpu.VMEM((2, rows, channels), BF16),
+                pltpu.VMEM(weights.shape, BF16),
+                pltpu.VMEM(tile_vals.shape, BF16),
+                pltpu.VMEM(send_rows.shape, jnp.int32),
+                pltpu.VMEM(send_count.shape, jnp.int32),
                 pltpu.SemaphoreType.DMA((4, chans)),
                 pltpu.SemaphoreType.DMA((4, chans)),
                 pltpu.SemaphoreType.DMA((exchanges, blocks)),
                 pltpu.SemaphoreType.DMA((exchanges, blocks)),
+                pltpu.SemaphoreType.DMA((8,)),
             ],
             compiler_params=pltpu.CompilerParams(
-                collective_id=0, has_side_effects=True, vmem_limit_bytes=44 * 1024 * 1024
+                collective_id=0, has_side_effects=True, vmem_limit_bytes=60 * 1024 * 1024
             ),
-        )(y_last, dy_last, weights, tile_vals, tile_cols, tile_mask, slot_row)
+        )(y_last, dy_last, weights, tile_vals, tile_cols, tile_mask, send_rows, send_count)
 
     return jax.shard_map(
         on_device,

time: 62.6 us -> 59.3 us (0.947)
  local copies, waits for them, and re-layouts: 6.81 us -> 2.26 us
  Pallas kernels: 54.7 us -> 56.2 us
    unnamed x16 -> x4, local copies, waits for them, and re-layouts: 5.94 us -> 2.26 us
    pallas_call x1, Pallas kernels: 54.7 us -> 56.2 us  [on_device(): pl.pallas_call(functools.partial(kernel, blocks, subs, chans, slots_each,...]
    squeeze x1 -> x0, local copies, waits for them, and re-layouts: 0.78 us -> none  [on_device(): slot_row = jnp.where(live, send_rows[0], -1).reshape(1, halo)]
where the time goes in v2:
time: 59.3 us; the launch traced here: 59.1 us
  Pallas kernels  56.2 us (95%)
  local copies, waits for them, and re-layouts  2.26 us (4%)
  between operations  0.65 us (1%)
    pallas_call x1, Pallas kernels, on_device(): pl.pallas_call(functools.partial(kernel, blocks, subs, chans, slots_each,...  56.2 us
    unnamed x4, local copies, waits for them, and re-layouts  2.26 us

profile of v2, /device:TPU:0, one launch (start us, length us, event | category | flops | bytes accessed | tf_op | source)
XLA Modules:
  0.0 59.1 jit_solution(3470791233269767212)
XLA Ops:
  0.6 56.2 %shard_map.95 = (bf16[2,64,512]{2,1,0:T(8,128)(2,1)}, f32[2,2,64,128]{3,2,1,0:T(8,128)}) custom-call(bf16[2,64,512]{2,1,0:T(8,128)(2,1)} %y_hbm.1, bf16[2,64,512]{2,1,0:T(8,128)(2,1)} %dy_hbm.1, bf16[2,2,128,128]{3,2,1,0:T(8,128)(2,1)} %weights_hbm.1, bf16[4,8,128,128]{3,2,1,0:T(8,128)(2,1)} %tiles_hbm.1, s32[4,8]{1,0:T(4,128)} %cols_ref.1, ...), custom_call_target="tpu_custom_call" | custom-call | tf_op jit(solution)/shard_map/pallas_call | solution.py:293
  56.9 0.0 copy-start
  56.9 1.6 %copy.12 = bf16[2,64,512]{2,1,0:T(8,128)(2,1)} copy(bf16[2,64,512]{2,1,0:T(8,128)(2,1)} %get-tuple-element.4) | data formatting | bytes 262144
  58.5 0.0 copy-done
  58.5 0.7 %copy.13 = f32[2,2,64,128]{3,2,1,0:T(8,128)} copy(f32[2,2,64,128]{3,2,1,0:T(8,128)S(1)} %copy-done) | data formatting | bytes 262144
Async XLA Ops:
  56.9 1.6 %copy-start = (f32[2,2,64,128]{3,2,1,0:T(8,128)S(1)}, f32[2,2,64,128]{3,2,1,0:T(8,128)}, u32[]{:S(2)}) copy-start(f32[2,2,64,128]{3,2,1,0:T(8,128)} %get-tuple-element.5) | copy-start | bytes 393220

commit v3 on v2

--- a/solution.py
+++ b/solution.py
@@ -182,12 +182,33 @@
 
     def weight_part(layer, which, moved, slope):
         square[...] = dot_tn(moved, slope)
-        at = (layer * 2 + which) * part
-        wpart[at : at + part, :] = square[mine, :]
-
-    used = 2 * layers * part
-    if used < wpart.shape[0]:
-        wpart[used:, :] = jnp.zeros((wpart.shape[0] - used, channels), F32)
+        wpart[layer, which * part : (which + 1) * part, :] = square[mine, :]
+
+    used = 2 * part
+    spare = wpart.shape[1] - used
+    if spare:
+        wpart[:, used:, :] = jnp.zeros((layers, spare, channels), F32)
+    own_piece = pl.ds(pl.multiple_of(me * rows_each, rows_each), rows_each)
+
+    def reduce_of(layer):
+        return copy_of(4 * layers + layer, wpart.at[layer], wsum.at[layer], 0, rows_each, True)
+
+    def spread_of(layer):
+        return copy_of(5 * layers + layer, wred.at[layer], wall.at[layer], 0, rows_each, False)
+
+    def start_reduce(layer):
+        start(reduce_of(layer))
+        wsum[layer, own_piece, :] = wpart[layer, own_piece, :]
+
+    def start_spread(layer):
+        finish(reduce_of(layer))
+        total = wsum[layer, :rows_each, :]
+        for piece in range(1, blocks):
+            total = total + wsum[layer, piece * rows_each : (piece + 1) * rows_each, :]
+        wred[layer] = total * factor
+        start(spread_of(layer))
+        wall[layer, own_piece, :] = wred[layer]
+
 
     held[0] = arrived(0)
     out[0] = dot(pick[...], held[0].astype(BF16)).astype(BF16)
@@ -234,6 +255,8 @@
         slopes[1] = (held[3] * held[5]).astype(BF16)
         held[2] += send_gradient(moves, dot_nt(slopes[1], second).astype(BF16))
         weight_part(layer, 1, msgs[1], slopes[1])
+        if pending is not None:
+            start_spread(layer + 1)
         msgs[0] = message(moves + 1, held[4])
         linear_one = dot(msgs[0], first)
         gate_one = sigmoid(linear_one)
@@ -246,30 +269,19 @@
         slopes[0] = (held[2] * held[5]).astype(BF16)
         held[3] += send_gradient(moves + 1, dot_nt(slopes[0], first).astype(BF16))
         weight_part(layer, 0, msgs[0], slopes[0])
+        start_reduce(layer)
         pending = moves + 1
         moves += 2
 
-    reduce_copy = copy_of(4 * layers, wpart, wsum, 0, rows_each, True)
-    start(reduce_copy)
-    own_piece = pl.ds(pl.multiple_of(me * rows_each, rows_each), rows_each)
-    wsum[own_piece, :] = wpart[own_piece, :]
     wide[...] = held[2].T
     grads_ref[0] = wide[mine, :].astype(BF16)
-    finish(reduce_copy)
-    total = wsum[:rows_each, :]
-    for piece in range(1, blocks):
-        total = total + wsum[piece * rows_each : (piece + 1) * rows_each, :]
-    wred[...] = total * factor
-    spread_copy = copy_of(4 * layers + 1, wred, wall, 0, rows_each, False)
-    start(spread_copy)
-    wall[own_piece, :] = wred[...]
+    start_spread(0)
     wide[...] = (held[3] + returned(pending)).T
     grads_ref[1] = wide[mine, :].astype(BF16)
-    finish(spread_copy)
-    for layer in range(layers):
+    for layer in reversed(range(layers)):
+        finish(spread_of(layer))
         for which in range(2):
-            at = (layer * 2 + which) * part
-            wgrads_ref[layer, which] = wall[at : at + part, :]
+            wgrads_ref[layer, which] = wall[layer, which * part : (which + 1) * part, :]
 
 
 def solution(mesh):
@@ -283,9 +295,9 @@
         channels = part * chans
         slots_each = send_rows.shape[2]
         halo = blocks * slots_each
-        rows_each = max(8, 2 * layers * part // blocks)
+        rows_each = max(8, 2 * part // blocks)
         pieces = blocks * rows_each
-        exchanges = 4 * layers + 2
+        exchanges = 6 * layers
         factor = 1.0 / math.sqrt(rows * blocks)
         vmem = pl.BlockSpec(memory_space=pltpu.VMEM)
         hbm = pl.BlockSpec(memory_space=pl.ANY)
@@ -308,10 +320,10 @@
                 pltpu.VMEM((2 * layers, halo, channels), BF16),
                 pltpu.VMEM((2 * layers, halo, channels), BF16),
                 pltpu.VMEM((2 * layers, halo, channels), BF16),
-                pltpu.VMEM((pieces, channels), F32),
-                pltpu.VMEM((pieces, channels), F32),
-                pltpu.VMEM((rows_each, channels), F32),
-                pltpu.VMEM((pieces, channels), F32),
+                pltpu.VMEM((layers, pieces, channels), F32),
+                pltpu.VMEM((layers, pieces, channels), F32),
+                pltpu.VMEM((layers, rows_each, channels), F32),
+                pltpu.VMEM((layers, pieces, channels), F32),
                 pltpu.VMEM((channels, channels), F32),
                 pltpu.VMEM((channels, rows), F32),
                 pltpu.VMEM((6, rows, channels), F32),

time: 59.3 us -> 59.5 us (level)
  no operation moved by 1% of the time
where the time goes in v3:
time: 59.5 us; the launch traced here: 59.4 us
  Pallas kernels  56.4 us (95%)
  local copies, waits for them, and re-layouts  2.26 us (4%)
  between operations  0.65 us (1%)
    pallas_call x1, Pallas kernels, on_device(): pl.pallas_call(functools.partial(kernel, blocks, subs, chans, slots_each,...  56.4 us
    unnamed x4, local copies, waits for them, and re-layouts  2.26 us

profile of v3, /device:TPU:0, one launch (start us, length us, event | category | flops | bytes accessed | tf_op | source)
XLA Modules:
  0.0 59.4 jit_solution(4278302992595746235)
XLA Ops:
  0.6 56.4 %shard_map.95 = (bf16[2,64,512]{2,1,0:T(8,128)(2,1)}, f32[2,2,64,128]{3,2,1,0:T(8,128)}) custom-call(bf16[2,64,512]{2,1,0:T(8,128)(2,1)} %y_hbm.1, bf16[2,64,512]{2,1,0:T(8,128)(2,1)} %dy_hbm.1, bf16[2,2,128,128]{3,2,1,0:T(8,128)(2,1)} %weights_hbm.1, bf16[4,8,128,128]{3,2,1,0:T(8,128)(2,1)} %tiles_hbm.1, s32[4,8]{1,0:T(4,128)} %cols_ref.1, ...), custom_call_target="tpu_custom_call" | custom-call | tf_op jit(solution)/shard_map/pallas_call | solution.py:305
  57.1 0.0 copy-start
  57.1 1.6 %copy.12 = bf16[2,64,512]{2,1,0:T(8,128)(2,1)} copy(bf16[2,64,512]{2,1,0:T(8,128)(2,1)} %get-tuple-element.4) | data formatting | bytes 262144
  58.7 0.0 copy-done
  58.7 0.7 %copy.13 = f32[2,2,64,128]{3,2,1,0:T(8,128)} copy(f32[2,2,64,128]{3,2,1,0:T(8,128)S(1)} %copy-done) | data formatting | bytes 262144
Async XLA Ops:
  57.1 1.6 %copy-start = (f32[2,2,64,128]{3,2,1,0:T(8,128)S(1)}, f32[2,2,64,128]{3,2,1,0:T(8,128)}, u32[]{:S(2)}) copy-start(f32[2,2,64,128]{3,2,1,0:T(8,128)} %get-tuple-element.5) | copy-start | bytes 393220
